TPU v7x, 256 devices: a whole 4x4x8 slice. The times are simulated.
256 devices in a mesh: prow: 8 (over x, core), pcol: 32 (over z, y).
Axes of the slice: x: 4, y: 4, z: 8, core: 2. Of those that a mesh axis runs over, the one named last changes fastest.
Arguments:
- matrix: bfloat16 [4, 8, 512, 1, 32, 512], P(None, 'prow', None, None, 'pcol'), may hold values from -6 to 6
- upper_inv: bfloat16 [2, 512, 512], replicated, may hold values from -4 to 4
- lower_inv: bfloat16 [2, 512, 512], replicated, may hold values from -4 to 4
- solution: bfloat16 [1, 32, 512], P(None, 'pcol'), may hold values from -0.046875 to 0.046875
- right_side: float32 [4, 8, 512], P(None, 'prow'), may hold values from -6 to 6
- diagonal_block_inverses: bfloat16 [1, 8, 512, 512], P(None, 'prow'), may hold values from -0.009765625 to 0.009765625
Outputs:
- updated: bfloat16 [4, 8, 512, 1, 32, 512], P(None, 'prow', None, None, 'pcol')
- residual: float32 [4, 8, 512], P(None, 'prow')
- precond: float32 [8, 512], replicated
All inputs are finite; a program needn't handle non-finite values.
Results may differ from a plain program's by a relative error of at most 0.0085.
Values may be sent and summed in bfloat16 or wider, within the bound.
A program may use at most 128 MiB of HBM per device.

v0:
```python
import jax
import jax.numpy as jnp
from jax import lax
from jax.sharding import PartitionSpec as P

PANELS = 2


def broadcast(value, axis, source):
    kept = jnp.where(lax.axis_index(axis) == source, value, 0).astype(value.dtype)
    return lax.psum(kept, axis)


def shards(matrix, upper_inv, lower_inv, solution, right_side, diagonal_block_inverses):
    rows_blk = matrix.shape[0]
    cols_blk = matrix.shape[3]
    blk_width = matrix.shape[2]
    row_processors = lax.axis_size("prow")
    col_devs = lax.axis_size("pcol")
    col_index = lax.axis_index("pcol")
    base_matrix = matrix.reshape(rows_blk * blk_width, cols_blk * blk_width)
    current = base_matrix
    for section in range(PANELS):
        col_local = section // col_devs
        local_row_block = section // row_processors
        upper_tri = jnp.triu(upper_inv[section])
        lower_tri = jnp.tril(lower_inv[section])
        column = current
        row_band = current[local_row_block * blk_width : (local_row_block + 1) * blk_width, :]
        factored = jnp.dot(column, upper_tri, preferred_element_type=jnp.float32).astype(
            jnp.bfloat16
        )
        left_panel = broadcast(factored, "pcol", section % col_devs)
        top_local = jnp.dot(lower_tri, row_band, preferred_element_type=jnp.float32).astype(
            jnp.bfloat16
        )
        top_panel = broadcast(top_local, "prow", section % row_processors)
        current = (
            current.astype(jnp.float32)
            - jnp.dot(left_panel, top_panel, preferred_element_type=jnp.float32)
        ).astype(jnp.bfloat16)
    partial_value = jnp.dot(
        base_matrix, solution.reshape(cols_blk * blk_width), preferred_element_type=jnp.float32
    )
    totals = lax.psum(partial_value, "pcol")
    residual = right_side.reshape(rows_blk * blk_width) - totals
    res_blocks = residual.reshape(rows_blk, blk_width)
    slot_count = diagonal_block_inverses.shape[0]
    inverses = diagonal_block_inverses.reshape(slot_count, blk_width, blk_width)
    solve_count = slot_count * row_processors
    col_blocks = base_matrix.reshape(rows_blk * blk_width, cols_blk, blk_width)

    def carry_forward(blk_id, state):
        accum, solved = state
        owner_row = blk_id % row_processors
        slot_id = blk_id // row_processors
        pending = lax.dynamic_slice_in_dim(accum, slot_id * blk_width, blk_width, 0)
        res_block = lax.dynamic_slice_in_dim(res_blocks, slot_id, 1, 0)[0]
        inv_block = inverses[0].astype(jnp.float32)
        row_total = lax.psum(pending, "pcol")
        local_value = jnp.dot(inv_block, res_block - row_total, precision=lax.Precision.HIGHEST)
        new_value = broadcast(local_value, "prow", owner_row)
        rounded = new_value.astype(jnp.bfloat16)
        has_col = col_index == blk_id % col_devs
        col_piece = col_blocks[:, 0, :]
        product = jnp.dot(col_piece, rounded, preferred_element_type=jnp.float32)
        accum = accum + jnp.where(has_col, product, jnp.zeros_like(product))
        solved = lax.dynamic_update_slice_in_dim(solved, new_value[None], blk_id, 0)
        return (accum, solved)

    start = (
        jnp.zeros((rows_blk * blk_width,), jnp.float32),
        jnp.zeros((solve_count, blk_width), jnp.float32),
    )
    precond = lax.fori_loop(0, solve_count, carry_forward, start)[1]
    return (current.reshape(matrix.shape), residual.reshape(right_side.shape), precond)


def solution(mesh):
    return jax.shard_map(
        shards,
        mesh=mesh,
        in_specs=(
            P(None, "prow", None, None, "pcol", None),
            P(),
            P(),
            P(None, "pcol", None),
            P(None, "prow", None),
            P(None, "prow", None, None),
        ),
        out_specs=(P(None, "prow", None, None, "pcol", None), P(None, "prow", None), P()),
        check_vma=False,
    )
```

profile of v0, /device:TPU:1, one launch (start us, length us, event | category | flops | bytes accessed | tf_op | source)
XLA Modules:
  0.0 947.7 jit_solution(12790687416914332410)
XLA Ops:
  7.3 2.6 fusion.5
  10.0 2.9 fusion.3
  12.9 0.6 fusion.32
  13.6 65.6 %psum.69 = f32[2048]{0:T(1024)S(1)} all-reduce(f32[2048]{0:T(1024)S(1)} %bitcast.79), channel_id=1, replica_groups=mesh['prow'=8,'pcol'=32] {'pcol'}, use_global_device_ids=true, to_apply=%region_4.5 | all-reduce | flops 2048 | bytes 16384 | tf_op jit(solution)/shard_map/psum | solution.py:45
  79.3 154.3 %all-reduce.5.cloned.1.call-done = bf16[2048,512]{0,1:T(8,128)(2,1)} async-done(((bf16[2048,512]{0,1:T(8,128)(2,1)}), bf16[2048,512]{0,1:T(8,128)(2,1)}) %all-reduce.5.cloned.1.call-update) | async-done | bytes 2097168 | tf_op jit(solution)/shard_map/psum | solution.py:11
  233.6 3.0 subtract_convert_fusion.1
  236.6 1.3 copy-done.7
  237.9 1.3 fusion.6
  239.2 4.3 fusion.4
  243.6 1.0 copy-done.2
  244.6 691.6 %while.19 = (s32[]{:T(128)}, f32[2048]{0:T(1024)S(1)}, f32[8,512]{1,0:T(8,128)}, s32[]{:T(128)}, f32[4,512]{1,0:T(4,128)S(1)}, /*index=5*/bf16[1,1,512,512]{3,2,...) while((s32[]{:T(128)}, f32[2048]{0:T(1024)S(1)}, ...), condition=%wide.region_8.9_spmd.clone, body=%wide.region_5.8_spmd.clone.sunk | while | flops 5253665 | bytes 2712061 | solution.py:75
  244.7 58.2 %psum.74 = f32[512]{0:T(512)S(1)} all-reduce(f32[512]{0:T(512)S(1)} %dynamic_slice.28), channel_id=1, replica_groups=mesh['prow'=8,'pcol'=32] {'pcol'}, use_global_device_ids=true, to_apply=%region_6.6 | all-reduce | flops 512 | bytes 4096 | tf_op jit(solution)/shard_map/while/body/eval_jaxpr/psum | solution.py:60
  302.9 0.5 fusion.59
  303.4 31.3 %psum.75 = f32[512]{0:T(512)S(1)} all-reduce(f32[512]{0:T(512)S(1)} %broadcast_select_fusion.5), channel_id=1, replica_groups=mesh['prow'=8,'pcol'=32] {'prow'}, use_global_device_ids=true, to_apply=%region_7.7 | all-reduce | flops 512 | bytes 4096 | tf_op jit(solution)/shard_map/while/body/eval_jaxpr/psum | solution.py:11
  334.7 0.6 fusion.60
  335.3 1.4 dynamic_update_slice.13
  336.7 55.7 %psum.74 = f32[512]{0:T(512)S(1)} all-reduce(f32[512]{0:T(512)S(1)} %dynamic_slice.28), channel_id=1, replica_groups=mesh['prow'=8,'pcol'=32] {'pcol'}, use_global_device_ids=true, to_apply=%region_6.6 | all-reduce | flops 512 | bytes 4096 | tf_op jit(solution)/shard_map/while/body/eval_jaxpr/psum | solution.py:60
  393.0 26.6 %psum.75 = f32[512]{0:T(512)S(1)} all-reduce(f32[512]{0:T(512)S(1)} %broadcast_select_fusion.5), channel_id=1, replica_groups=mesh['prow'=8,'pcol'=32] {'prow'}, use_global_device_ids=true, to_apply=%region_7.7 | all-reduce | flops 512 | bytes 4096 | tf_op jit(solution)/shard_map/while/body/eval_jaxpr/psum | solution.py:11
  419.6 0.6 fusion.60
  420.3 1.4 dynamic_update_slice.13
  421.7 57.8 %psum.74 = f32[512]{0:T(512)S(1)} all-reduce(f32[512]{0:T(512)S(1)} %dynamic_slice.28), channel_id=1, replica_groups=mesh['prow'=8,'pcol'=32] {'pcol'}, use_global_device_ids=true, to_apply=%region_6.6 | all-reduce | flops 512 | bytes 4096 | tf_op jit(solution)/shard_map/while/body/eval_jaxpr/psum | solution.py:60
  480.0 26.6 %psum.75 = f32[512]{0:T(512)S(1)} all-reduce(f32[512]{0:T(512)S(1)} %broadcast_select_fusion.5), channel_id=1, replica_groups=mesh['prow'=8,'pcol'=32] {'prow'}, use_global_device_ids=true, to_apply=%region_7.7 | all-reduce | flops 512 | bytes 4096 | tf_op jit(solution)/shard_map/while/body/eval_jaxpr/psum | solution.py:11
  506.7 0.6 fusion.60
  507.3 1.4 dynamic_update_slice.13
  508.7 55.7 %psum.74 = f32[512]{0:T(512)S(1)} all-reduce(f32[512]{0:T(512)S(1)} %dynamic_slice.28), channel_id=1, replica_groups=mesh['prow'=8,'pcol'=32] {'pcol'}, use_global_device_ids=true, to_apply=%region_6.6 | all-reduce | flops 512 | bytes 4096 | tf_op jit(solution)/shard_map/while/body/eval_jaxpr/psum | solution.py:60
  564.5 0.5 fusion.59
  565.0 26.6 %psum.75 = f32[512]{0:T(512)S(1)} all-reduce(f32[512]{0:T(512)S(1)} %broadcast_select_fusion.5), channel_id=1, replica_groups=mesh['prow'=8,'pcol'=32] {'prow'}, use_global_device_ids=true, to_apply=%region_7.7 | all-reduce | flops 512 | bytes 4096 | tf_op jit(solution)/shard_map/while/body/eval_jaxpr/psum | solution.py:11
  591.5 0.6 fusion.60
  592.2 1.4 dynamic_update_slice.13
  593.6 57.2 %psum.74 = f32[512]{0:T(512)S(1)} all-reduce(f32[512]{0:T(512)S(1)} %dynamic_slice.28), channel_id=1, replica_groups=mesh['prow'=8,'pcol'=32] {'pcol'}, use_global_device_ids=true, to_apply=%region_6.6 | all-reduce | flops 512 | bytes 4096 | tf_op jit(solution)/shard_map/while/body/eval_jaxpr/psum | solution.py:60
  651.3 26.6 %psum.75 = f32[512]{0:T(512)S(1)} all-reduce(f32[512]{0:T(512)S(1)} %broadcast_select_fusion.5), channel_id=1, replica_groups=mesh['prow'=8,'pcol'=32] {'prow'}, use_global_device_ids=true, to_apply=%region_7.7 | all-reduce | flops 512 | bytes 4096 | tf_op jit(solution)/shard_map/while/body/eval_jaxpr/psum | solution.py:11
  678.0 0.6 fusion.60
  678.6 1.4 dynamic_update_slice.13
  680.0 55.7 %psum.74 = f32[512]{0:T(512)S(1)} all-reduce(f32[512]{0:T(512)S(1)} %dynamic_slice.28), channel_id=1, replica_groups=mesh['prow'=8,'pcol'=32] {'pcol'}, use_global_device_ids=true, to_apply=%region_6.6 | all-reduce | flops 512 | bytes 4096 | tf_op jit(solution)/shard_map/while/body/eval_jaxpr/psum | solution.py:60
  736.3 26.6 %psum.75 = f32[512]{0:T(512)S(1)} all-reduce(f32[512]{0:T(512)S(1)} %broadcast_select_fusion.5), channel_id=1, replica_groups=mesh['prow'=8,'pcol'=32] {'prow'}, use_global_device_ids=true, to_apply=%region_7.7 | all-reduce | flops 512 | bytes 4096 | tf_op jit(solution)/shard_map/while/body/eval_jaxpr/psum | solution.py:11
  762.9 0.6 fusion.60
  763.5 1.4 dynamic_update_slice.13
  764.9 57.2 %psum.74 = f32[512]{0:T(512)S(1)} all-reduce(f32[512]{0:T(512)S(1)} %dynamic_slice.28), channel_id=1, replica_groups=mesh['prow'=8,'pcol'=32] {'pcol'}, use_global_device_ids=true, to_apply=%region_6.6 | all-reduce | flops 512 | bytes 4096 | tf_op jit(solution)/shard_map/while/body/eval_jaxpr/psum | solution.py:60
  822.1 0.5 fusion.59
  822.6 26.6 %psum.75 = f32[512]{0:T(512)S(1)} all-reduce(f32[512]{0:T(512)S(1)} %broadcast_select_fusion.5), channel_id=1, replica_groups=mesh['prow'=8,'pcol'=32] {'prow'}, use_global_device_ids=true, to_apply=%region_7.7 | all-reduce | flops 512 | bytes 4096 | tf_op jit(solution)/shard_map/while/body/eval_jaxpr/psum | solution.py:11
  849.3 0.6 fusion.60
  849.9 1.4 dynamic_update_slice.13
  851.3 55.7 %psum.74 = f32[512]{0:T(512)S(1)} all-reduce(f32[512]{0:T(512)S(1)} %dynamic_slice.28), channel_id=1, replica_groups=mesh['prow'=8,'pcol'=32] {'pcol'}, use_global_device_ids=true, to_apply=%region_6.6 | all-reduce | flops 512 | bytes 4096 | tf_op jit(solution)/shard_map/while/body/eval_jaxpr/psum | solution.py:60
  907.1 0.5 fusion.59
  907.6 26.6 %psum.75 = f32[512]{0:T(512)S(1)} all-reduce(f32[512]{0:T(512)S(1)} %broadcast_select_fusion.5), channel_id=1, replica_groups=mesh['prow'=8,'pcol'=32] {'prow'}, use_global_device_ids=true, to_apply=%region_7.7 | all-reduce | flops 512 | bytes 4096 | tf_op jit(solution)/shard_map/while/body/eval_jaxpr/psum | solution.py:11
  934.2 0.6 fusion.60
  934.8 1.4 dynamic_update_slice.13
  936.2 5.0 subtract_convert_fusion
  (98 shorter events, 3.3 us)
Async XLA Ops:
  7.2 5.8 copy-start
  7.2 2.8 copy-start.1
  7.2 2.8 copy-start.6
  7.2 72.0 %all-reduce.7.cloned.1.call-start = ((), (), s32[]{:S(2)}) async-start(), calls=%async_computation.1 | async-start | bytes 1048576 | tf_op jit(solution)/shard_map/psum | solution.py:11
  9.9 223.7 %all-reduce.5.cloned.1.call-start = ((), (), s32[]{:S(2)}) async-start(), calls=%async_computation | async-start | bytes 4194304 | tf_op jit(solution)/shard_map/psum | solution.py:11
  12.8 66.3 %copy-start.4 = (f32[4,1,512]{2,1,0:T(1,128)S(1)}, f32[4,1,512]{2,1,0:T(1,128)}, u32[]{:S(2)}) copy-start(f32[4,1,512]{2,1,0:T(1,128)} %param.12) | copy-start | bytes 24580
  12.9 923.3 %all-reduce.11.cloned.1.call-start = ((), (), s32[]{:S(2)}) async-start(), calls=%async_computation.3 | async-start | bytes 1048576 | tf_op jit(solution)/shard_map/psum | solution.py:11
  79.2 157.4 %copy-start.3 = (f32[2048]{0:T(1024)}, f32[2048]{0:T(1024)S(1)}, u32[]{:S(2)}) copy-start(f32[2048]{0:T(1024)S(1)} %sub.28) | copy-start | bytes 24580
  79.2 158.7 %copy-start.5 = (bf16[2,512,512]{2,1,0:T(8,128)(2,1)S(1)}, bf16[2,512,512]{2,1,0:T(8,128)(2,1)}, u32[]{:S(2)}) copy-start(bf16[2,512,512]{2,1,0:T(8,128)(2,1)} %param.10) | copy-start | bytes 3145732
  236.6 1.3 copy-start.7
  239.2 697.0 %all-reduce.9.cloned.1.call-start = ((), (), s32[]{:S(2)}) async-start(), calls=%async_computation.2 | async-start | bytes 4194304 | tf_op jit(solution)/shard_map/psum | solution.py:11
  243.6 1.0 copy-start.2
Sparse Core Ops, SparseCore 0:
  10.4 67.5 all-reduce.6
  82.5 151.0 all-reduce.4
  239.3 64.9 all-reduce.10
  308.1 151.9 all-reduce.8
where the time goes:
time: 949 us; the launch traced here: 948 us
  blocking collectives  736 us (78%)
  waiting for transfers between devices  154 us (16%)
  matrix products  28.7 us (3%)
  local copies, waits for them, and re-layouts  13.9 us (1%)
  between operations  13.9 us (1%)
    psum x8, blocking collectives, carry_forward(): row_total = lax.psum(pending, 'pcol')  453 us
    psum x8, blocking collectives, broadcast(): return lax.psum(kept, axis)  217 us
    psum x4, waiting for transfers between devices, broadcast(): return lax.psum(kept, axis)  154 us
    psum x1, blocking collectives, shards(): totals = lax.psum(partial_value, 'pcol')  65.6 us
  transfers between devices with their start and end apart: 4, of which 1 were waited for; matrix products, arithmetic and copies ran while one was open for 3% of the time, Pallas kernels for 0%

commit v1 on v0

--- a/solution.py
+++ b/solution.py
@@ -57,7 +57,11 @@
         pending = lax.dynamic_slice_in_dim(accum, slot_id * blk_width, blk_width, 0)
         res_block = lax.dynamic_slice_in_dim(res_blocks, slot_id, 1, 0)[0]
         inv_block = inverses[0].astype(jnp.float32)
-        row_total = lax.psum(pending, "pcol")
+        row_total = pending
+        for hop in (1, 2, 4, 8, 16):
+            row_total = row_total + lax.ppermute(
+                row_total, "pcol", [(dev, dev ^ hop) for dev in range(32)]
+            )
         local_value = jnp.dot(inv_block, res_block - row_total, precision=lax.Precision.HIGHEST)
         new_value = broadcast(local_value, "prow", owner_row)
         rounded = new_value.astype(jnp.bfloat16)

time: 949 us -> 792 us (0.83)
  blocking collectives: 736 us -> 208 us
  waiting for transfers between devices: 154 us -> 482 us
  starting transfers between devices: 0.16 us -> 43.1 us
    psum x8 -> x0, blocking collectives: 453 us -> none  [carry_forward(): row_total = lax.psum(pending, 'pcol')]
    psum x4, waiting for transfers between devices: 154 us -> 376 us  [broadcast(): return lax.psum(kept, axis)]
    ppermute x0 -> x40, waiting for transfers between devices: none -> 106 us  [carry_forward(): lax.ppermute(row_total, 'pcol', [(dev, dev ^ hop) for dev in range(32)])]
    psum x8, blocking collectives: 217 us -> 149 us  [broadcast(): return lax.psum(kept, axis)]
    ppermute x0 -> x40, starting transfers between devices: none -> 43 us  [carry_forward(): lax.ppermute(row_total, 'pcol', [(dev, dev ^ hop) for dev in range(32)])]
  transfers between devices with their start and end apart: 4 -> 44, of which waited for: 1 -> 44; matrix products, arithmetic and copies ran while one was open for 3% -> 1% of each run, Pallas kernels for 0% -> 0%
where the time goes in v1:
time: 792 us; the launch traced here: 790 us
  waiting for transfers between devices  482 us (61%)
  blocking collectives  208 us (26%)
  starting transfers between devices  43.1 us (5%)
  matrix products  28.7 us (4%)
  between operations  13.9 us (2%)
  local copies, waits for them, and re-layouts  12.9 us (2%)
    psum x4, waiting for transfers between devices, broadcast(): return lax.psum(kept, axis)  376 us
    psum x8, blocking collectives, broadcast(): return lax.psum(kept, axis)  149 us
    ppermute x40, waiting for transfers between devices, carry_forward(): lax.ppermute(row_total, 'pcol', [(dev, dev ^ hop) for dev in range(32)])  106 us
    psum x1, blocking collectives, shards(): totals = lax.psum(partial_value, 'pcol')  59.2 us
    ppermute x40, starting transfers between devices, carry_forward(): lax.ppermute(row_total, 'pcol', [(dev, dev ^ hop) for dev in range(32)])  43 us
  transfers between devices with their start and end apart: 44, of which 44 were waited for; matrix products, arithmetic and copies ran while one was open for 1% of the time, Pallas kernels for 0%

profile of v1, /device:TPU:1, one launch (start us, length us, event | category | flops | bytes accessed | tf_op | source)
XLA Modules:
  0.0 790.5 jit_solution(3818912720331743034)
XLA Ops:
  7.3 2.6 fusion.5
  10.0 2.9 fusion.3
  12.9 65.0 %all-reduce.7.cloned.1.call-done = bf16[512,512]{1,0:T(8,128)(2,1)} async-done(((bf16[512,512]{1,0:T(8,128)(2,1)}), bf16[512,512]{1,0:T(8,128)(2,1)}) %all-reduce.7.cloned.1.call-update) | async-done | bytes 524304 | tf_op jit(solution)/shard_map/psum | solution.py:11
  77.9 155.7 %all-reduce.5.cloned.1.call-done = bf16[2048,512]{0,1:T(8,128)(2,1)} async-done(((bf16[2048,512]{0,1:T(8,128)(2,1)}), bf16[2048,512]{0,1:T(8,128)(2,1)}) %all-reduce.5.cloned.1.call-update) | async-done | bytes 2097168 | tf_op jit(solution)/shard_map/psum | solution.py:11
  233.6 3.0 subtract_convert_fusion.1
  239.2 4.3 fusion.4
  244.2 59.2 %psum.54 = f32[2048]{0:T(1024)S(1)} all-reduce(f32[2048]{0:T(1024)S(1)} %bitcast.79), channel_id=1, replica_groups=mesh['prow'=8,'pcol'=32] {'pcol'}, use_global_device_ids=true, to_apply=%region_4.5 | all-reduce | flops 2048 | bytes 16384 | tf_op jit(solution)/shard_map/psum | solution.py:45
  304.3 154.9 %all-reduce.9.cloned.1.call-done = bf16[2048,512]{1,0:T(8,128)(2,1)} async-done(((bf16[2048,512]{1,0:T(8,128)(2,1)}), bf16[2048,512]{1,0:T(8,128)(2,1)}) %all-reduce.9.cloned.1.call-update) | async-done | bytes 2097168 | tf_op jit(solution)/shard_map/psum | solution.py:11
  459.2 5.0 subtract_convert_fusion
  464.2 319.7 %while.19 = (s32[]{:T(128)}, f32[2048]{0:T(1024)S(1)}, f32[8,512]{1,0:T(8,128)}, s32[]{:T(128)}, f32[4,512]{1,0:T(4,128)S(1)}, /*index=5*/bf16[1,1,512,512]{3,2,...) while((s32[]{:T(128)}, f32[2048]{0:T(1024)S(1)}, ...), condition=%wide.region_7.8_spmd.clone, body=%wide.region_5.7_spmd.clone.sunk | while | flops 5255713 | bytes 2775761 | solution.py:79
  476.6 3.3 collective-permute-start.4
  479.9 3.0 collective-permute-done.4
  483.4 22.7 %psum.57 = f32[512]{0:T(512)S(1)} all-reduce(f32[512]{0:T(512)S(1)} %broadcast_select_fusion.5), channel_id=1, replica_groups=mesh['prow'=8,'pcol'=32] {'prow'}, use_global_device_ids=true, to_apply=%region_6.6 | all-reduce | flops 512 | bytes 4096 | tf_op jit(solution)/shard_map/while/body/eval_jaxpr/psum | solution.py:11
  508.3 2.4 collective-permute-done
  511.9 2.8 collective-permute-done.1
  520.6 2.6 collective-permute-start.4
  523.2 3.7 collective-permute-done.4
  527.5 18.1 %psum.57 = f32[512]{0:T(512)S(1)} all-reduce(f32[512]{0:T(512)S(1)} %broadcast_select_fusion.5), channel_id=1, replica_groups=mesh['prow'=8,'pcol'=32] {'prow'}, use_global_device_ids=true, to_apply=%region_6.6 | all-reduce | flops 512 | bytes 4096 | tf_op jit(solution)/shard_map/while/body/eval_jaxpr/psum | solution.py:11
  547.7 2.4 collective-permute-done
  551.3 2.8 collective-permute-done.1
  560.0 2.6 collective-permute-start.4
  562.6 3.7 collective-permute-done.4
  566.9 18.1 %psum.57 = f32[512]{0:T(512)S(1)} all-reduce(f32[512]{0:T(512)S(1)} %broadcast_select_fusion.5), channel_id=1, replica_groups=mesh['prow'=8,'pcol'=32] {'prow'}, use_global_device_ids=true, to_apply=%region_6.6 | all-reduce | flops 512 | bytes 4096 | tf_op jit(solution)/shard_map/while/body/eval_jaxpr/psum | solution.py:11
  587.1 2.4 collective-permute-done
  590.7 2.8 collective-permute-done.1
  599.4 2.6 collective-permute-start.4
  602.0 3.7 collective-permute-done.4
  606.3 18.1 %psum.57 = f32[512]{0:T(512)S(1)} all-reduce(f32[512]{0:T(512)S(1)} %broadcast_select_fusion.5), channel_id=1, replica_groups=mesh['prow'=8,'pcol'=32] {'prow'}, use_global_device_ids=true, to_apply=%region_6.6 | all-reduce | flops 512 | bytes 4096 | tf_op jit(solution)/shard_map/while/body/eval_jaxpr/psum | solution.py:11
  626.5 2.4 collective-permute-done
  630.1 2.8 collective-permute-done.1
  638.8 2.6 collective-permute-start.4
  641.4 3.7 collective-permute-done.4
  645.7 18.1 %psum.57 = f32[512]{0:T(512)S(1)} all-reduce(f32[512]{0:T(512)S(1)} %broadcast_select_fusion.5), channel_id=1, replica_groups=mesh['prow'=8,'pcol'=32] {'prow'}, use_global_device_ids=true, to_apply=%region_6.6 | all-reduce | flops 512 | bytes 4096 | tf_op jit(solution)/shard_map/while/body/eval_jaxpr/psum | solution.py:11
  665.9 2.4 collective-permute-done
  669.5 2.8 collective-permute-done.1
  678.2 2.6 collective-permute-start.4
  680.8 3.7 collective-permute-done.4
  685.1 18.1 %psum.57 = f32[512]{0:T(512)S(1)} all-reduce(f32[512]{0:T(512)S(1)} %broadcast_select_fusion.5), channel_id=1, replica_groups=mesh['prow'=8,'pcol'=32] {'prow'}, use_global_device_ids=true, to_apply=%region_6.6 | all-reduce | flops 512 | bytes 4096 | tf_op jit(solution)/shard_map/while/body/eval_jaxpr/psum | solution.py:11
  705.3 2.4 collective-permute-done
  708.9 2.8 collective-permute-done.1
  717.6 2.6 collective-permute-start.4
  720.3 3.7 collective-permute-done.4
  724.5 18.1 %psum.57 = f32[512]{0:T(512)S(1)} all-reduce(f32[512]{0:T(512)S(1)} %broadcast_select_fusion.5), channel_id=1, replica_groups=mesh['prow'=8,'pcol'=32] {'prow'}, use_global_device_ids=true, to_apply=%region_6.6 | all-reduce | flops 512 | bytes 4096 | tf_op jit(solution)/shard_map/while/body/eval_jaxpr/psum | solution.py:11
  744.7 2.4 collective-permute-done
  748.3 2.8 collective-permute-done.1
  757.0 2.6 collective-permute-start.4
  759.7 3.7 collective-permute-done.4
  763.9 18.1 %psum.57 = f32[512]{0:T(512)S(1)} all-reduce(f32[512]{0:T(512)S(1)} %broadcast_select_fusion.5), channel_id=1, replica_groups=mesh['prow'=8,'pcol'=32] {'prow'}, use_global_device_ids=true, to_apply=%region_6.6 | all-reduce | flops 512 | bytes 4096 | tf_op jit(solution)/shard_map/while/body/eval_jaxpr/psum | solution.py:11
  (202 shorter events, 87.4 us)
Async XLA Ops:
  7.2 236.4 %copy-start = (bf16[1,1,512]{2,1,0:T(2,128)(2,1)S(1)}, bf16[1,1,512]{2,1,0:T(2,128)(2,1)}, u32[]{:S(2)}) copy-start(bf16[1,1,512]{2,1,0:T(2,128)(2,1)} %param.11) | copy-start | bytes 3076
  7.2 70.7 %all-reduce.7.cloned.1.call-start = ((), (), s32[]{:S(2)}) async-start(), calls=%async_computation.1 | async-start | bytes 1048576 | tf_op jit(solution)/shard_map/psum | solution.py:11
  9.9 223.7 %all-reduce.5.cloned.1.call-start = ((), (), s32[]{:S(2)}) async-start(), calls=%async_computation | async-start | bytes 4194304 | tf_op jit(solution)/shard_map/psum | solution.py:11
  12.9 291.5 %all-reduce.11.cloned.1.call-start = ((), (), s32[]{:S(2)}) async-start(), calls=%async_computation.3 | async-start | bytes 1048576 | tf_op jit(solution)/shard_map/psum | solution.py:11
  12.9 225.0 %copy-start.5 = (bf16[2,512,512]{2,1,0:T(8,128)(2,1)S(1)}, bf16[2,512,512]{2,1,0:T(8,128)(2,1)}, u32[]{:S(2)}) copy-start(bf16[2,512,512]{2,1,0:T(8,128)(2,1)} %param.10) | copy-start | bytes 3145732
  239.2 220.1 %all-reduce.9.cloned.1.call-start = ((), (), s32[]{:S(2)}) async-start(), calls=%async_computation.2 | async-start | bytes 4194304 | tf_op jit(solution)/shard_map/psum | solution.py:11
  303.4 160.8 %copy-start.3 = (f32[2048]{0:T(1024)}, f32[2048]{0:T(1024)S(1)}, u32[]{:S(2)}) copy-start(f32[2048]{0:T(1024)S(1)} %sub.28) | copy-start | bytes 24580
  303.5 160.8 %copy-start.2 = (bf16[1,1,512,512]{3,2,1,0:T(8,128)(2,1)S(1)}, bf16[1,1,512,512]{3,2,1,0:T(8,128)(2,1)}, u32[]{:S(2)}) copy-start(bf16[1,1,512,512]{3,2,1,0:T(8,128)(2,1)} %param.13) | copy-start | bytes 1572868
  464.3 2.5 collective-permute-start
  466.8 4.0 collective-permute-start.1
  470.8 2.4 collective-permute-start.2
  473.3 3.3 collective-permute-start.3
  476.6 6.3 collective-permute-start.4
  508.2 2.5 collective-permute-start
  510.8 4.0 collective-permute-start.1
  514.7 2.5 collective-permute-start.2
  517.3 3.3 collective-permute-start.3
  520.6 6.3 collective-permute-start.4
  547.6 2.5 collective-permute-start
  550.2 4.0 collective-permute-start.1
  554.1 2.5 collective-permute-start.2
  556.7 3.3 collective-permute-start.3
  560.0 6.3 collective-permute-start.4
  587.0 2.5 collective-permute-start
  589.6 4.0 collective-permute-start.1
  593.5 2.5 collective-permute-start.2
  596.1 3.3 collective-permute-start.3
  599.4 6.3 collective-permute-start.4
  626.4 2.5 collective-permute-start
  629.0 4.0 collective-permute-start.1
  632.9 2.5 collective-permute-start.2
  635.5 3.3 collective-permute-start.3
  638.8 6.3 collective-permute-start.4
  665.8 2.5 collective-permute-start
  668.4 4.0 collective-permute-start.1
  672.3 2.5 collective-permute-start.2
  674.9 3.3 collective-permute-start.3
  678.2 6.3 collective-permute-start.4
  705.2 2.5 collective-permute-start
  707.8 4.0 collective-permute-start.1
  711.7 2.5 collective-permute-start.2
  714.3 3.3 collective-permute-start.3
  717.6 6.3 collective-permute-start.4
  744.6 2.5 collective-permute-start
  747.2 4.0 collective-permute-start.1
  751.1 2.5 collective-permute-start.2
  753.7 3.3 collective-permute-start.3
  757.0 6.3 collective-permute-start.4
  (4 other events, 66.7 us)
Sparse Core Ops, SparseCore 0:
  10.4 67.4 all-reduce.6
  82.4 151.1 all-reduce.4
  239.3 64.9 all-reduce.10
  308.1 151.0 all-reduce.8
